TPU v7x, 128 devices: a whole 4x4x4 slice. The times are simulated.
128 devices in a mesh: grp: 4 (over y), shard: 32 (over x, z, core).
Axes of the slice: x: 4, y: 4, z: 4, core: 2. Of those that a mesh axis runs over, the one named last changes fastest.
Arguments:
- new_rows: bfloat16 [32768, 1024], P(('grp', 'shard'))
- cluster_ids: int32 [32768], P(('grp', 'shard')), may hold values from 0 to 7, as said below
- new_order: int32 [32768], P(('grp', 'shard')), may hold values from 0 to 2147483646
- codes: bfloat16 [8, 8192, 1024], P('grp', 'shard'), may hold values from -8 to 8
- scales: float32 [8, 1024], P('grp')
- offsets: float32 [8, 1024], P('grp')
- counts: int32 [8], P('grp'), may hold values from 1024 to 8192, as said below
- earlier_order: int32 [8, 8192], P('grp', 'shard'), may hold values from 1 to 2147483646
Outputs:
- max_similarity: float32 [32768], P(('grp', 'shard'))
Inputs may be any that keep to these rules, and one draw needn't show every extreme that they name: `cluster_ids`: in each device's block of 256 rows, no group's clusters are named by more than 128 rows, and some group's clusters are named by exactly 128 rows. `counts`: some cluster has all 8192 slots live.
All inputs are finite; a program needn't handle non-finite values.
Results may differ from a plain program's by a relative error of at most 0.00047.
Values may be sent and summed in bfloat16 or wider, within the bound.
A program may use at most 128 MiB of HBM per device.

v0:
```python
import jax
import jax.numpy as jnp
from jax import lax
from jax.sharding import PartitionSpec as P

epsilon = 1e-06


def unit_rows(values):
    return (values / jnp.sqrt(jnp.sum(values * values, axis=-1, keepdims=True) + epsilon)).astype(
        jnp.bfloat16
    )


def score_clusters(
    running, queries, query_cluster, query_order, key_source, key_order, live_counts, prepare
):
    width = key_source.shape[1]
    positions = jnp.arange(width, dtype=jnp.int32)
    best = running
    for cluster in range(key_source.shape[0]):
        cluster_keys = prepare(key_source[cluster], cluster)
        scores = jnp.dot(queries, cluster_keys.T, preferred_element_type=jnp.float32)
        allowed = (
            (query_cluster[:, None] == cluster)
            & (positions[None, :] < live_counts[cluster])
            & (key_order[cluster][None, :] < query_order[:, None])
        )
        best = jnp.maximum(best, jnp.max(jnp.where(allowed, scores, -1.0), axis=1))
    return best


def per_device(new_rows, cluster_ids, new_order, codes, scales, offsets, counts, earlier_order):
    groups = lax.axis_size("grp")
    owned_count = codes.shape[0]
    local_rows = new_rows.shape[0]
    capacity = local_rows // 2
    queries = unit_rows(new_rows.astype(jnp.float32))
    target = cluster_ids // owned_count
    onehot = (target[:, None] == jnp.arange(groups, dtype=jnp.int32)[None, :]).astype(jnp.int32)
    slot_rank = jnp.sum((jnp.cumsum(onehot, axis=0) - onehot) * onehot, axis=1)
    position = target * capacity + slot_rank
    received = groups * capacity
    matches = position[None, :] == jnp.arange(received, dtype=jnp.int32)[:, None]
    filled = jnp.any(matches, axis=1)
    source_row = jnp.sum(
        jnp.where(matches, jnp.arange(local_rows, dtype=jnp.int32)[None, :], 0), axis=1
    )
    send_rows = jnp.take(queries, source_row, axis=0).reshape(groups, capacity, queries.shape[1])
    send_cluster = jnp.where(filled, jnp.take(cluster_ids % owned_count, source_row), 0).reshape(
        groups, capacity
    )
    send_order = jnp.where(filled, jnp.take(new_order, source_row), 0).reshape(groups, capacity)
    got_rows, got_cluster, got_order = (
        lax.all_to_all(send_rows, "grp", split_axis=0, concat_axis=0, tiled=True),
        lax.all_to_all(send_cluster, "grp", split_axis=0, concat_axis=0, tiled=True),
        lax.all_to_all(send_order, "grp", split_axis=0, concat_axis=0, tiled=True),
    )
    got_rows = got_rows.reshape(received, queries.shape[1])
    got_cluster = got_cluster.reshape(received)
    got_order = got_order.reshape(received)
    starting = jnp.zeros((received,), jnp.float32)

    def decode_one(code_rows, cluster):
        return unit_rows(
            code_rows.astype(jnp.float32) * scales[cluster][None, :] + offsets[cluster][None, :]
        )

    top_score = score_clusters(
        starting,
        got_rows,
        got_cluster,
        got_order,
        lax.all_gather(codes, "shard", axis=1, tiled=True),
        lax.all_gather(earlier_order, "shard", axis=1, tiled=True),
        counts,
        decode_one,
    )
    answered = lax.all_to_all(
        top_score.reshape(groups, capacity), "grp", split_axis=0, concat_axis=0, tiled=True
    )
    return jnp.take(answered.reshape(received), position)


def solution(mesh):
    return jax.shard_map(
        per_device,
        mesh=mesh,
        in_specs=(
            P(("grp", "shard"), None),
            P(("grp", "shard")),
            P(("grp", "shard")),
            P("grp", "shard", None),
            P("grp", None),
            P("grp", None),
            P("grp"),
            P("grp", "shard"),
        ),
        out_specs=P(("grp", "shard")),
        check_vma=False,
    )
```

profile of v0, /device:TPU:0, one launch (start us, length us, event | category | flops | bytes accessed | tf_op | source)
XLA Modules:
  0.0 194.7 jit_solution(17353483784496994221)
XLA Ops:
  6.5 0.7 all-gather.2.cloned.1.call-update
  7.3 0.7 and_select_fusion
  8.0 1.2 reduce-window.6
  10.3 3.5 %gather_fusion.2 = s32[512]{0:T(512)S(1)} fusion(s32[256]{0:T(256)S(1)} %get-tuple-element.20, s32[1024]{0:T(1024)S(1)} %pad_clamp_fusion.2), kind=kCustom, calls=%fused_computation.clone | custom fusion | bytes 6144 | tf_op jit(solution)/shard_map/jit(_take)/gather | solution.py:50
  13.9 3.5 %gather_fusion.3 = s32[512]{0:T(512)S(1)} fusion(s32[256]{0:T(256)S(1)} %copy-done, s32[1024]{0:T(1024)S(1)} %pad_clamp_fusion.2), kind=kCustom, calls=%fused_computation.1.clone | custom fusion | bytes 6144 | tf_op jit(solution)/shard_map/jit(_take)/gather | solution.py:53
  18.1 4.5 %all-to-all-start = ((s32[4,1,128]{2,1,0:T(1,128)}), s32[4,1,128]{2,1,0:T(1,128)S(1)}, u32[]{:S(2)}, u32[]{:S(2)}) async-start(s32[4,1,128]{2,1,0:T(1,128)} %bitcast.3), calls=%async_computation | async-start | bytes 4096 | tf_op jit(solution)/shard_map/all_to_all | solution.py:56
  22.7 1.3 fusion.26
  24.0 1.4 fusion.27
  25.3 2.1 %gather_fusion = bf16[512,1024]{1,0:T(8,128)(2,1)S(1)} fusion(bf16[256,1024]{1,0:T(8,128)(2,1)S(1)} %fusion.27, s32[1024]{0:T(1024)S(1)} %pad_clamp_fusion.1), kind=kCustom, calls=%fused_computation.2 | custom fusion | bytes 2099200 | tf_op jit(solution)/shard_map/jit(_take)/gather | solution.py:49
  27.4 25.5 %all_gather.6 = s32[2,8192]{1,0:T(2,128)S(1)} all-gather(s32[2,256]{1,0:T(2,128)} %param.17), channel_id=1, replica_groups=mesh['grp'=4,'shard'=32] {'shard'}, dimensions={1}, use_global_device_ids=true | all-gather | bytes 67584 | tf_op jit(solution)/shard_map/all_gather | solution.py:75
  52.9 1.3 fusion.35
  54.9 0.8 fusion.33
  55.7 0.8 fusion.34
  56.5 1.2 broadcast_select_fusion
  58.2 4.7 %all-to-all-start.1 = ((s32[4,1,128]{2,1,0:T(1,128)}), s32[4,1,128]{2,1,0:T(1,128)S(1)}, u32[]{:S(2)}, u32[]{:S(2)}) async-start(s32[4,1,128]{2,1,0:T(1,128)} %bitcast.6), calls=%async_computation.1 | async-start | bytes 4096 | tf_op jit(solution)/shard_map/all_to_all | solution.py:57
  63.0 5.2 %all-to-all-done.1 = s32[4,1,128]{2,1,0:T(1,128)S(1)} async-done(((s32[4,1,128]{2,1,0:T(1,128)}), s32[4,1,128]{2,1,0:T(1,128)S(1)}, u32[]{:S(2)}, u32[]{:S(2)}) %all-to-all-start.1) | async-done | bytes 2080 | tf_op jit(solution)/shard_map/all_to_all | solution.py:57
  68.2 3.5 %all-to-all-start.2 = ((bf16[4,128,1024]{2,1,0:T(8,128)(2,1)}), bf16[4,128,1024]{2,1,0:T(8,128)(2,1)S(1)}, u32[]{:S(2)}, u32[]{:S(2)}) async-start(bf16[4,128,1024]{2,1,0:T(8,128)(2,1)} %broadcast_select_fusion), calls=%async_computation.2 | async-start | bytes 2097152 | tf_op jit(solution)/shard_map/all_to_all | solution.py:55
  71.8 54.4 %all-gather.2.cloned.1.call-done = bf16[2,8192,1024]{2,1,0:T(8,128)(2,1)} async-done(((bf16[2,256,1024]{2,1,0:T(8,128)(2,1)}), bf16[2,8192,1024]{2,1,0:T(8,128)(2,1)}) %all-gather.2.cloned.1.call-update) | async-done | bytes 33554448 | tf_op jit(solution)/shard_map/all_gather | solution.py:74
  126.2 20.2 %fusion.6 = (f32[8192]{0:T(1024)S(1)}, f32[8192]{0:T(1024)S(1)}) fusion(f32[1024]{0:T(1024)S(1)} %bitcast.89, f32[1024]{0:T(1024)S(1)} %bitcast.87, bf16[2,8192,1024]{2,1,0:T(8,128)(2,1)} %all-gather.2.cloned.1.call-done, f32[1024]{0:T(1024)S(1)} %bitcast.85, f32[1024]{0:T(1024)S(1)} %bitcast.83), kind=kLoop, calls=%fused_computation.14 | loop fusion | flops 83869696 | bytes 33636352 | tf_op jit(solution)/shard_map/reduce_sum | solution.py:10
  146.4 14.4 %select_reduce_fusion.1 = f32[512]{0:T(512)S(1)} fusion(s32[8192]{0:T(1024)S(1)} %bitcast.81, s32[512]{0:T(512)S(1)} %bitcast.93, pred[8192]{0:T(1024)(128)(4,1)S(1)} %iota_compare_fusion.2, pred[512]{0:T(512)(128)(4,1)S(1)} %bitcast.96, bf16[512,1024]{1,0:T(8,128)(2,1)S(1)} %bitcast.77, f32[8192]{0:T(1024)S(1)} %get-tuple-element.25, ...), kind=kOutput, calls=%fused_computation.25 | convolution fusion | flops 8652849152 | bytes 17912320 | tf_op jit(solution)/shard_map/dot_general | solution.py:23
  160.9 14.5 %select_reduce_fusion = f32[512]{0:T(512)S(1)} fusion(s32[8192]{0:T(1024)S(1)} %bitcast.80, s32[512]{0:T(512)S(1)} %bitcast.94, pred[8192]{0:T(1024)(128)(4,1)S(1)} %iota_compare_fusion.1, pred[512]{0:T(512)(128)(4,1)S(1)} %bitcast.95, bf16[512,1024]{1,0:T(8,128)(2,1)S(1)} %bitcast.78, f32[8192]{0:T(1024)S(1)} %get-tuple-element.24, f32[1024]{0:T(1024)S(1)} %bitcast.86, ...), kind=kOutput, calls=%fused_computation.24 | convolution fusion | flops 8652849152 | bytes 17912320 | tf_op jit(solution)/shard_map/dot_general | solution.py:23
  175.9 4.3 %all-to-all-start.3 = ((f32[4,1,128]{2,1,0:T(1,128)}), f32[4,1,128]{2,1,0:T(1,128)S(1)}, u32[]{:S(2)}, u32[]{:S(2)}) async-start(f32[4,1,128]{2,1,0:T(1,128)} %bitcast.23), calls=%async_computation.3 | async-start | bytes 4096 | tf_op jit(solution)/shard_map/all_to_all | solution.py:79
  180.2 5.1 %all-to-all-done.3 = f32[4,1,128]{2,1,0:T(1,128)S(1)} async-done(((f32[4,1,128]{2,1,0:T(1,128)}), f32[4,1,128]{2,1,0:T(1,128)S(1)}, u32[]{:S(2)}, u32[]{:S(2)}) %all-to-all-start.3) | async-done | bytes 2080 | tf_op jit(solution)/shard_map/all_to_all | solution.py:79
  185.3 1.9 gather_fusion.1
  (37 shorter events, 4.4 us)
Async XLA Ops:
  6.5 7.3 %copy-start = (s32[256]{0:T(256)S(1)}, s32[256]{0:T(256)}, u32[]{:S(2)}) copy-start(s32[256]{0:T(256)} %param.12) | copy-start | bytes 3076
  6.5 119.7 %all-gather.2.cloned.1.call-start = ((), (), s32[]{:S(2)}) async-start(), calls=%async_computation.4 | async-start | bytes 34603008 | tf_op jit(solution)/shard_map/all_gather | solution.py:74
  10.2 13.8 %copy-start.1 = (s32[256]{0:T(256)}, s32[256]{0:T(256)S(1)}, u32[]{:S(2)}) copy-start(s32[256]{0:T(256)S(1)} %get-tuple-element.11) | copy-start | bytes 3076
  18.1 40.1 %all-to-all-start = ((s32[4,1,128]{2,1,0:T(1,128)}), s32[4,1,128]{2,1,0:T(1,128)S(1)}, u32[]{:S(2)}, u32[]{:S(2)}) async-start(s32[4,1,128]{2,1,0:T(1,128)} %bitcast.3), calls=%async_computation | async-start | bytes 4096 | tf_op jit(solution)/shard_map/all_to_all | solution.py:56
  58.2 10.0 %all-to-all-start.1 = ((s32[4,1,128]{2,1,0:T(1,128)}), s32[4,1,128]{2,1,0:T(1,128)S(1)}, u32[]{:S(2)}, u32[]{:S(2)}) async-start(s32[4,1,128]{2,1,0:T(1,128)} %bitcast.6), calls=%async_computation.1 | async-start | bytes 4096 | tf_op jit(solution)/shard_map/all_to_all | solution.py:57
  68.2 78.2 %all-to-all-start.2 = ((bf16[4,128,1024]{2,1,0:T(8,128)(2,1)}), bf16[4,128,1024]{2,1,0:T(8,128)(2,1)S(1)}, u32[]{:S(2)}, u32[]{:S(2)}) async-start(bf16[4,128,1024]{2,1,0:T(8,128)(2,1)} %broadcast_select_fusion), calls=%async_computation.2 | async-start | bytes 2097152 | tf_op jit(solution)/shard_map/all_to_all | solution.py:55
  160.8 19.4 %copy-start.3 = (s32[256]{0:T(256)S(1)}, s32[256]{0:T(256)}, u32[]{:S(2)}) copy-start(s32[256]{0:T(256)} %get-tuple-element.10) | copy-start | bytes 3076
  160.8 26.4 %copy-start.2 = (s32[256]{0:T(256)S(1)}, s32[256]{0:T(256)}, u32[]{:S(2)}) copy-start(s32[256]{0:T(256)} %copy-done.1) | copy-start | bytes 3076
  175.9 9.4 %all-to-all-start.3 = ((f32[4,1,128]{2,1,0:T(1,128)}), f32[4,1,128]{2,1,0:T(1,128)S(1)}, u32[]{:S(2)}, u32[]{:S(2)}) async-start(f32[4,1,128]{2,1,0:T(1,128)} %bitcast.23), calls=%async_computation.3 | async-start | bytes 4096 | tf_op jit(solution)/shard_map/all_to_all | solution.py:79
Sparse Core Ops, SparseCore 0:
  9.7 116.4 all-gather.1
where the time goes:
time: 195 us
  waiting for transfers between devices  65.5 us (34%)
  other arithmetic  29.9 us (15%)
  matrix products  28.9 us (15%)
  blocking collectives  25.5 us (13%)
  starting transfers between devices  17.1 us (9%)
  local copies, waits for them, and re-layouts  14.3 us (7%)
  between operations  13.6 us (7%)
    all_gather x1, waiting for transfers between devices, per_device(): lax.all_gather(codes, 'shard', axis=1, tiled=True)  54.4 us
    dot_general x2, matrix products, score_clusters(): jnp.dot(queries, cluster_keys.T, preferred_element_type=jnp.float32)  28.9 us
    all_gather x1, blocking collectives, per_device(): lax.all_gather(earlier_order, 'shard', axis=1, tiled=True)  25.5 us
    reduce_sum x2, other arithmetic, unit_rows(): jnp.sum(values * values, axis=-1, keepdims=True) + epsilon  21.4 us
    all_to_all x1, waiting for transfers between devices, per_device(): lax.all_to_all(send_order, 'grp', split_axis=0, concat_axis=0, tiled=True)  5.23 us
    all_to_all x1, waiting for transfers between devices, per_device(): lax.all_to_all(top_score.reshape(groups, capacity), 'grp', split_axis=0,...  5.09 us
    all_to_all x1, starting transfers between devices, per_device(): lax.all_to_all(send_order, 'grp', split_axis=0, concat_axis=0, tiled=True)  4.72 us
    all_to_all x1, starting transfers between devices, per_device(): lax.all_to_all(send_cluster, 'grp', split_axis=0, concat_axis=0, tiled=True)  4.55 us
  transfers between devices with their start and end apart: 5, of which 3 were waited for; matrix products, arithmetic and copies ran while one was open for 21% of the time, Pallas kernels for 0%

commit v1 on v0

--- a/solution.py
+++ b/solution.py
@@ -71,7 +71,9 @@
         got_rows,
         got_cluster,
         got_order,
-        lax.all_gather(codes, "shard", axis=1, tiled=True),
+        jnp.concatenate(
+            lax.all_to_all(jnp.stack([codes] * lax.axis_size("shard")), "shard", 0, 0), axis=1
+        ),
         lax.all_gather(earlier_order, "shard", axis=1, tiled=True),
         counts,
         decode_one,

time: 195 us -> 704 us (3.61)
  blocking collectives: 25.5 us -> 568 us
  waiting for transfers between devices: 65.5 us -> 5.1 us
  other arithmetic: 29.9 us -> 55.7 us
  between operations: 13.6 us -> 0.26 us
  local copies, waits for them, and re-layouts: 14.3 us -> 23.8 us
    all_gather x1, blocking collectives: 25.5 us -> 558 us  [per_device(): lax.all_gather(earlier_order, 'shard', axis=1, tiled=True)]
    all_gather x1 -> x0, waiting for transfers between devices: 54.4 us -> none  [per_device(): lax.all_gather(codes, 'shard', axis=1, tiled=True)]
    convert_element_type x1 -> x2, other arithmetic: 1.36 us -> 28.6 us  [unit_rows(): (values / jnp.sqrt(jnp.sum(values * values, axis=-1, keepdims=True) + eps...]
    another operation x2 -> x3, local copies, waits for them, and re-layouts: 0.1 us -> 11.9 us  [the longest x1 11.8 us: per_device(): jnp.stack([codes] * lax.axis_size('shard'))]
    all_to_all x0 -> x1, blocking collectives: none -> 9.59 us  [per_device(): lax.all_to_all(send_cluster, 'grp', split_axis=0, concat_axis=0, tiled=True)]
  transfers between devices with their start and end apart: 5 -> 4, of which waited for: 3 -> 1; matrix products, arithmetic and copies ran while one was open for 21% -> 8% of each run, Pallas kernels for 0% -> 0%
where the time goes in v1:
time: 704 us; the launch traced here: 701 us
  blocking collectives  568 us (81%)
  other arithmetic  55.7 us (8%)
  matrix products  27.3 us (4%)
  local copies, waits for them, and re-layouts  23.8 us (3%)
  starting transfers between devices  21.2 us (3%)
    all_gather x1, blocking collectives, per_device(): lax.all_gather(earlier_order, 'shard', axis=1, tiled=True)  558 us
    convert_element_type x2, other arithmetic, unit_rows(): (values / jnp.sqrt(jnp.sum(values * values, axis=-1, keepdims=True) + eps...  28.6 us
    dot_general x2, matrix products, score_clusters(): jnp.dot(queries, cluster_keys.T, preferred_element_type=jnp.float32)  27.3 us
    reduce_sum x2, other arithmetic, unit_rows(): jnp.sum(values * values, axis=-1, keepdims=True) + epsilon  20.5 us
  transfers between devices with their start and end apart: 4, of which 1 were waited for; matrix products, arithmetic and copies ran while one was open for 8% of the time, Pallas kernels for 0%

profile of v1, /device:TPU:0, one launch (start us, length us, event | category | flops | bytes accessed | tf_op | source)
XLA Modules:
  0.0 701.3 jit_solution(5184262825892293871)
XLA Ops:
  0.0 0.7 and_select_fusion
  0.7 1.2 reduce-window.6
  2.7 3.5 gather_fusion.2
  6.2 3.5 gather_fusion.3
  9.8 0.6 select_select_fusion.1
  10.4 9.6 %all_to_all.34 = s32[4,1,128]{2,1,0:T(1,128)S(1)} all-to-all(s32[4,1,128]{2,1,0:T(1,128)S(1)} %bitcast.69), channel_id=1, replica_groups=mesh['grp'=4,'shard'=32] {'grp'}, dimensions={0} | all-to-all | bytes 4096 | tf_op jit(solution)/shard_map/all_to_all | solution.py:56
  19.9 11.8 %stack.2 = bf16[32,2,256,1024]{3,2,1,0:T(8,128)(2,1)} broadcast(bf16[2,256,1024]{2,1,0:T(8,128)(2,1)} %param.13), dimensions={1,2,3} | broadcast | bytes 34603008 | tf_op jit(solution)/shard_map/stack | solution.py:75
  31.8 8.4 %all-to-all-start.3 = ((bf16[32,2,256,1024]{3,2,1,0:T(8,128)(2,1)}), bf16[32,2,256,1024]{3,2,1,0:T(8,128)(2,1)}, u32[]{:S(2)}, u32[]{:S(2)}) async-start(bf16[32,2,256,1024]{3,2,1,0:T(8,128)(2,1)} %stack.2), calls=%async_computation.3 | async-start | bytes 67108864 | tf_op jit(solution)/shard_map/all_to_all | solution.py:75
  40.7 2.1 gather_fusion
  42.7 558.4 %all_gather.3 = s32[2,8192]{1,0:T(2,128)S(1)} all-gather(s32[2,256]{1,0:T(2,128)S(1)} %copy-done.5), channel_id=1, replica_groups=mesh['grp'=4,'shard'=32] {'shard'}, dimensions={1}, use_global_device_ids=true | all-gather | bytes 67584 | tf_op jit(solution)/shard_map/all_gather | solution.py:77
  601.1 0.6 fusion.9
  601.7 0.7 iota_compare_fusion.2
  602.4 0.6 iota_compare_fusion.1
  603.0 1.1 broadcast_select_fusion
  604.2 3.2 all-to-all-start.1
  607.4 20.3 %multiply_reduce_fusion.1 = (f32[32,256]{1,0:T(8,128)S(1)}, f32[32,256]{1,0:T(8,128)S(1)}) fusion(f32[1024]{0:T(1024)S(1)} %bitcast.63, f32[1024]{0:T(1024)S(1)} %bitcast.59, bf16[2,32,256,1024]{3,2,0,1:T(8,128)(2,1)} %bitcast.13, f32[1024]{0:T(1024)S(1)} %bitcast.61, f32[1024]{0:T(1024)S(1)} %bitcast.57), kind=kLoop, calls=%fused_computation.8 | loop fusion | flops 83869696 | bytes 33636352 | tf_op jit(solution)/shard_map/reduce_sum | solution.py:10
  627.8 4.8 all-to-all-start.2
  632.6 28.4 %divide_convert_fusion.1 = (bf16[1,32,256,1024]{3,2,0,1:T(8,128)(2,1)}, bf16[1,32,256,1024]{3,2,0,1:T(8,128)(2,1)}) fusion(f32[32,256]{1,0:T(8,128)S(1)} %get-tuple-element.27, f32[1024]{0:T(1024)S(1)} %bitcast.64, f32[1024]{0:T(1024)S(1)} %bitcast.60, bf16[2,32,256,1024]{3,2,0,1:T(8,128)(2,1)} %bitcast.13, f32[32,256]{1,0:T(8,128)S(1)} %get-tuple-element.26, ...), kind=kLoop, calls=%fused_computation.7 | loop fusion | flops 83886080 | bytes 67190784 | tf_op jit(solution)/shard_map/convert_element_type | solution.py:10
  661.0 13.6 %select_reduce_fusion.1 = f32[512]{0:T(512)S(1)} fusion(bf16[512,1024]{1,0:T(8,128)(2,1)S(1)} %bitcast.54, bf16[8192,1024]{1,0:T(8,128)(2,1)} %bitcast.52, s32[8192]{0:T(1024)S(1)} %bitcast.66, s32[512]{0:T(512)S(1)} %bitcast.71, pred[8192]{0:T(1024)(128)(4,1)S(1)} %iota_compare_fusion.2, pred[512]{0:T(512)(128)(4,1)S(1)} %bitcast.74), kind=kOutput, calls=%fused_computation.11 | convolution fusion | flops 8610906112 | bytes 17871360 | tf_op jit(solution)/shard_map/dot_general | solution.py:23
  674.6 13.7 %select_reduce_fusion = f32[512]{0:T(512)S(1)} fusion(bf16[512,1024]{1,0:T(8,128)(2,1)S(1)} %bitcast.55, bf16[8192,1024]{1,0:T(8,128)(2,1)} %bitcast.51, s32[8192]{0:T(1024)S(1)} %bitcast.65, s32[512]{0:T(512)S(1)} %bitcast.72, pred[8192]{0:T(1024)(128)(4,1)S(1)} %iota_compare_fusion.1, pred[512]{0:T(512)(128)(4,1)S(1)} %bitcast.73), kind=kOutput, calls=%fused_computation.10 | convolution fusion | flops 8610906112 | bytes 17871360 | tf_op jit(solution)/shard_map/dot_general | solution.py:23
  688.3 0.6 maximum_maximum_fusion
  688.9 4.8 all-to-all-start.4
  693.7 5.1 all-to-all-done.4
  698.8 1.9 gather_fusion.1
  (43 shorter events, 1.9 us)
Async XLA Ops:
  0.0 6.2 copy-start
  31.7 8.5 %copy-start.2 = (bf16[256,1024]{1,0:T(8,128)(2,1)S(1)}, bf16[256,1024]{1,0:T(8,128)(2,1)}, u32[]{:S(2)}) copy-start(bf16[256,1024]{1,0:T(8,128)(2,1)} %param.10) | copy-start | bytes 1572868
  31.7 11.0 %copy-start.5 = (s32[2,256]{1,0:T(2,128)S(1)}, s32[2,256]{1,0:T(2,128)}, u32[]{:S(2)}) copy-start(s32[2,256]{1,0:T(2,128)} %param.17) | copy-start | bytes 6148
  31.7 569.4 %copy-start.6 = (s32[2]{0:T(128)S(1)}, s32[2]{0:T(128)}, u32[]{:S(2)}) copy-start(s32[2]{0:T(128)} %param.16) | copy-start | bytes 28
  31.7 571.2 %copy-start.3 = (f32[2,1024]{1,0:T(2,128)S(1)}, f32[2,1024]{1,0:T(2,128)}, u32[]{:S(2)}) copy-start(f32[2,1024]{1,0:T(2,128)} %param.14) | copy-start | bytes 24580
  31.8 571.2 %copy-start.4 = (f32[2,1024]{1,0:T(2,128)S(1)}, f32[2,1024]{1,0:T(2,128)}, u32[]{:S(2)}) copy-start(f32[2,1024]{1,0:T(2,128)} %param.15) | copy-start | bytes 24580
  31.8 572.5 %all-to-all-start.3 = ((bf16[32,2,256,1024]{3,2,1,0:T(8,128)(2,1)}), bf16[32,2,256,1024]{3,2,1,0:T(8,128)(2,1)}, u32[]{:S(2)}, u32[]{:S(2)}) async-start(bf16[32,2,256,1024]{3,2,1,0:T(8,128)(2,1)} %stack.2), calls=%async_computation.3 | async-start | bytes 67108864 | tf_op jit(solution)/shard_map/all_to_all | solution.py:75
  604.2 23.5 %all-to-all-start.1 = ((s32[4,1,128]{2,1,0:T(1,128)}), s32[4,1,128]{2,1,0:T(1,128)S(1)}, u32[]{:S(2)}, u32[]{:S(2)}) async-start(s32[4,1,128]{2,1,0:T(1,128)} %bitcast.6), calls=%async_computation.1 | async-start | bytes 4096 | tf_op jit(solution)/shard_map/all_to_all | solution.py:57
  627.8 33.2 %all-to-all-start.2 = ((bf16[4,128,1024]{2,1,0:T(8,128)(2,1)}), bf16[4,128,1024]{2,1,0:T(8,128)(2,1)S(1)}, u32[]{:S(2)}, u32[]{:S(2)}) async-start(bf16[4,128,1024]{2,1,0:T(8,128)(2,1)} %broadcast_select_fusion), calls=%async_computation.2 | async-start | bytes 2097152 | tf_op jit(solution)/shard_map/all_to_all | solution.py:55
  674.6 26.7 %copy-start.1 = (s32[256]{0:T(256)S(1)}, s32[256]{0:T(256)}, u32[]{:S(2)}) copy-start(s32[256]{0:T(256)} %param.12) | copy-start | bytes 3076
  688.9 9.9 %all-to-all-start.4 = ((f32[4,1,128]{2,1,0:T(1,128)}), f32[4,1,128]{2,1,0:T(1,128)S(1)}, u32[]{:S(2)}, u32[]{:S(2)}) async-start(f32[4,1,128]{2,1,0:T(1,128)} %bitcast.22), calls=%async_computation.4 | async-start | bytes 4096 | tf_op jit(solution)/shard_map/all_to_all | solution.py:81
